TPU v7x, 32 devices: a whole 2x2x4 slice. The times are simulated.
32 devices in a mesh: seq: 8 (over y, x, core), batch: 4 (over z).
Axes of the slice: x: 2, y: 2, z: 4, core: 2. Of those that a mesh axis runs over, the one named last changes fastest.
Arguments:
- ssm_input: bfloat16 [8192, 4096], P(('batch', 'seq')), parts along dimension 0, may hold values from -6 to 6
- gate_input: bfloat16 [8192, 4096], P(('batch', 'seq')), parts along dimension 0, may hold values from -6 to 6
- b_rows: bfloat16 [8192, 128], P(('batch', 'seq')), parts along dimension 0, may hold values from -6 to 6
- c_rows: bfloat16 [8192, 128], P(('batch', 'seq')), parts along dimension 0, may hold values from -6 to 6
- step_raw: float32 [8192, 64], P(('batch', 'seq')), parts along dimension 0, may hold values from -14 to 2
- step_bias: float32 [64], replicated, may hold values from -0.5 to 0.5
- rate_log: float32 [64], replicated, may hold values from -1.5 to 4
- skip_gain: float32 [64], replicated, may hold values from 0.5 to 2
- norm_gain: float32 [4096], replicated, may hold values from 0.5 to 1.5
- w_out: bfloat16 [4096, 4096], P(None, 'seq'), may hold values from -0.09375 to 0.09375
- residual: bfloat16 [8192, 4096], P(('batch', 'seq')), parts along dimension 0, may hold values from -6 to 6
- moe_gain: float32 [4096], replicated, may hold values from 0.5 to 1.5
- router: bfloat16 [4096, 8], replicated, may hold values from -0.09375 to 0.09375
- expert_ids: int32 [8192, 2], P(('batch', 'seq')), parts along dimension 0, may hold values from 0 to 7, all different within a row; in each aligned block of 256 rows (0 to 255, 256 to 511, ...) at most 96 rows name the same one
- w_gate: bfloat16 [8, 4096, 384], P('seq'), may hold values from -0.09375 to 0.09375
- w_up: bfloat16 [8, 4096, 384], P('seq'), may hold values from -0.09375 to 0.09375
- w_down: bfloat16 [8, 384, 4096], P('seq'), may hold values from -0.3125 to 0.3125
Outputs:
- layer_out: bfloat16 [8192, 4096], P(('batch', 'seq')), parts along dimension 0
There are 4 independent parts, one for each index of `batch`. A program takes and returns all parts, laid end to end along the dimension named above; an argument that names none is the same for every part. Nothing has to cross between parts.
Inputs may be any that keep to these rules, and one draw needn't show every extreme that they name: `expert_ids`: the 2 ids of a token differ. In the rows of one device (256 rows, aligned blocks), no expert is named by more than 96 rows, a bound that some block reaches.
All inputs are finite; a program needn't handle non-finite values.
Results may differ from a plain program's by a relative error of at most 0.008.
Values may be sent and summed in bfloat16 or wider, within the bound.
A program may use at most 192 MiB of HBM per device.

v0:
```python
import jax
import jax.numpy as jnp
from jax import lax
from jax.sharding import PartitionSpec as P

GROUP = 256


def group_pass(carried, pieces):
    inputs, b_block, c_block, steps_h, logs_h = pieces
    running = jnp.cumsum(logs_h, axis=0)
    length = logs_h.shape[0]
    scores = jnp.dot(c_block, b_block.T, preferred_element_type=jnp.float32)
    causal = jnp.arange(length)[:, None] >= jnp.arange(length)[None, :]
    spread = running[:, None, :] - running[None, :, :]
    decays = jnp.exp(jnp.where(causal[:, :, None], spread, -jnp.inf))
    mixing = (scores[:, :, None] * decays * steps_h[None, :, :]).astype(jnp.bfloat16)
    intra = jnp.einsum("tsh,shp->thp", mixing, inputs, preferred_element_type=jnp.float32)
    c_wide = c_block.astype(jnp.float32)
    from_state = jnp.exp(running)[:, :, None] * jnp.einsum(
        "tn,hpn->thp", c_wide, carried, precision=lax.Precision.HIGHEST
    )
    departing_state = jnp.exp(running[-1][None, :] - running) * steps_h
    block_in = (departing_state[:, :, None] * b_block.astype(jnp.float32)[:, None, :]).astype(
        jnp.bfloat16
    )
    update = jnp.einsum("shn,shp->hpn", block_in, inputs, preferred_element_type=jnp.float32)
    new_carried = jnp.exp(running[-1])[:, None, None] * carried + update
    return (new_carried, intra + from_state)


def shards(
    ssm_input,
    gate_input,
    b_rows,
    c_rows,
    step_raw,
    step_bias,
    rate_log,
    skip_gain,
    norm_gain,
    w_out,
    residual,
    moe_gain,
    router,
    expert_ids,
    w_gate,
    w_up,
    w_down,
):
    tokens_here = ssm_input.shape[0]
    inner = ssm_input.shape[1]
    heads = rate_log.shape[0]
    head_width = inner // heads
    state_width = b_rows.shape[1]
    blocks = tokens_here // GROUP
    step_sizes = jax.nn.softplus(step_raw + step_bias[None, :])
    log_decay = -step_sizes * jnp.exp(rate_log)[None, :]
    inputs = ssm_input.reshape(tokens_here, heads, head_width)
    pieces = (
        inputs.reshape(blocks, GROUP, heads, head_width),
        b_rows.reshape(blocks, GROUP, state_width),
        c_rows.reshape(blocks, GROUP, state_width),
        step_sizes.reshape(blocks, GROUP, heads),
        log_decay.reshape(blocks, GROUP, heads),
    )
    start = jnp.zeros((heads, head_width, state_width), jnp.float32)
    segment_state, outputs = lax.scan(group_pass, start, pieces)
    slab_log = jnp.cumsum(log_decay, axis=0)
    slab_total = slab_log[-1]
    all_logs, every_state_list = (
        lax.all_gather(slab_total[None], "seq", axis=0, tiled=True),
        lax.all_gather(segment_state[None], "seq", axis=0, tiled=True),
    )
    position = lax.axis_index("seq")
    through = jnp.cumsum(all_logs, axis=0)
    before_me = lax.dynamic_index_in_dim(through - all_logs, position, 0, keepdims=False)
    earlier = (jnp.arange(all_logs.shape[0]) < position)[:, None]
    weights = jnp.exp(jnp.where(earlier, before_me[None, :] - through, -jnp.inf))
    entering = jnp.einsum(
        "jh,jhpn->hpn", weights, every_state_list, precision=lax.Precision.HIGHEST
    )
    c_wide = c_rows.astype(jnp.float32)
    arriving = jnp.exp(slab_log)[:, :, None] * jnp.einsum(
        "tn,hpn->thp", c_wide, entering, precision=lax.Precision.HIGHEST
    )
    ssm_out = (
        outputs.reshape(tokens_here, heads, head_width)
        + arriving
        + skip_gain[None, :, None] * inputs.astype(jnp.float32)
    )
    gated = ssm_out.reshape(tokens_here, inner) * jax.nn.silu(gate_input.astype(jnp.float32))
    normed = (
        gated
        * lax.rsqrt(jnp.mean(gated * gated, axis=1, keepdims=True) + 1e-05)
        * norm_gain[None, :]
    ).astype(jnp.bfloat16)
    columns = jnp.dot(
        lax.all_gather(normed, "seq", axis=0, tiled=True), w_out, preferred_element_type=jnp.float32
    ).astype(jnp.bfloat16)
    mixer_out = lax.all_to_all(columns, "seq", split_axis=0, concat_axis=1, tiled=True)
    hidden = (residual.astype(jnp.float32) + mixer_out.astype(jnp.float32)).astype(jnp.bfloat16)
    hidden_wide = hidden.astype(jnp.float32)
    moe_input = (
        hidden_wide
        * lax.rsqrt(jnp.mean(hidden_wide * hidden_wide, axis=1, keepdims=True) + 1e-05)
        * moe_gain[None, :]
    ).astype(jnp.bfloat16)
    logits = jnp.dot(moe_input, router, preferred_element_type=jnp.float32)
    chosen = jnp.take_along_axis(logits, expert_ids, axis=1)
    powers = jnp.exp(chosen)
    combine = powers / jnp.sum(powers, axis=1, keepdims=True)
    experts_all = lax.axis_size("seq")
    fanout = expert_ids.shape[1]
    capacity = tokens_here * fanout * 3 // (2 * experts_all)
    width = moe_input.shape[1]
    flat_ids = expert_ids.reshape(-1)
    one_hot = (flat_ids[:, None] == jnp.arange(experts_all, dtype=jnp.int32)[None, :]).astype(
        jnp.int32
    )
    running_count = jnp.cumsum(one_hot, axis=0)
    slot_of = jnp.sum(running_count * one_hot, axis=1) - 1
    target = flat_ids * capacity + slot_of
    repeated = jnp.repeat(moe_input, fanout, axis=0)
    departing_state = (
        jnp.zeros((experts_all * capacity, width), jnp.bfloat16).at[target].set(repeated)
    )
    departing_state = departing_state.reshape(experts_all, capacity, width)
    batch = lax.all_to_all(departing_state, "seq", split_axis=0, concat_axis=0, tiled=True)
    flat_rows = batch.reshape(-1, width)
    gate_part = jnp.dot(flat_rows, w_gate[0], preferred_element_type=jnp.float32)
    up_part = jnp.dot(flat_rows, w_up[0], preferred_element_type=jnp.float32)
    expert_hidden = (jax.nn.silu(gate_part) * up_part).astype(jnp.bfloat16)
    result = jnp.dot(expert_hidden, w_down[0], preferred_element_type=jnp.float32).astype(
        jnp.bfloat16
    )
    finished = result.reshape(batch.shape)
    returned = lax.all_to_all(finished, "seq", split_axis=0, concat_axis=0, tiled=True).reshape(
        experts_all * capacity, width
    )
    fetched = returned[target].astype(jnp.float32).reshape(tokens_here, fanout, width)
    total = hidden_wide + jnp.sum(combine[:, :, None] * fetched, axis=1)
    return total.astype(jnp.bfloat16)


def solution(mesh):
    in_specs = (
        P(("batch", "seq"), None),
        P(("batch", "seq"), None),
        P(("batch", "seq"), None),
        P(("batch", "seq"), None),
        P(("batch", "seq"), None),
        P(),
        P(),
        P(),
        P(),
        P(None, "seq"),
        P(("batch", "seq"), None),
        P(),
        P(),
        P(("batch", "seq"), None),
        P("seq", None, None),
        P("seq", None, None),
        P("seq", None, None),
    )
    out_specs = P(("batch", "seq"), None)
    return jax.shard_map(shards, mesh=mesh, in_specs=in_specs, out_specs=out_specs, check_vma=False)
```

profile of v0, /device:TPU:0, one launch (start us, length us, event | category | flops | bytes accessed | tf_op | source)
XLA Modules:
  0.0 541.9 jit_solution(18407337214512243547)
XLA Ops:
  6.5 0.8 exp.45
  7.4 1.1 multiply_bitcast_fusion
  8.5 0.6 reduce-window.16
  9.1 0.2 slice_reduce_fusion
  9.3 0.1 bitcast_bitcast_fusion
  9.4 0.2 slice_reduce_fusion.1
  9.6 0.8 fusion.45
  10.4 4.1 copy.38
  14.5 5.1 add_bitcast_fusion
  19.7 10.2 %all-gather.1 = f32[8,1,64]{2,1,0:T(1,128)S(1)} all-gather(f32[1,1,64]{2,1,0:T(1,128)S(1)} %bitcast.118), channel_id=1, replica_groups=mesh['seq'=8,'batch'=4] {'seq'}, dimensions={0}, use_global_device_ids=true | all-gather | bytes 2304 | tf_op jit(solution)/shard_map/all_gather | solution.py:72
  30.0 0.7 copy.49
  30.7 0.6 iota_compare_fusion
  31.4 0.2 fusion.47
  31.6 3.7 fusion.36
  35.3 77.1 %all-gather.7.cloned.1.call-done = f32[512,64,128]{2,1,0:T(8,128)} async-done(((f32[64,64,128]{2,1,0:T(8,128)}), f32[512,64,128]{2,1,0:T(8,128)}) %all-gather.7.cloned.1.call-update) | async-done | bytes 16777232 | tf_op jit(solution)/shard_map/all_gather | solution.py:73
  112.4 30.3 %fusion = f32[64,1,64,128]{3,1,2,0:T(1,128)S(1)} fusion(f32[8,64,1,1]{0,2,3,1:T(1,128)S(1)} %copy-done.17, f32[8,64,64,128]{3,2,1,0:T(8,128)} %bitcast.102), kind=kOutput, calls=%fused_computation.3 | convolution fusion | flops 50331648 | bytes 18876416 | tf_op jit(solution)/shard_map/jh,jhpn->hpn/dot_general | solution.py:80
  142.8 1.8 fusion.38
  144.6 0.3 copy-done.8
  144.9 0.7 copy-done.10
  145.6 6.6 %fusion.19 = f32[256,64,64]{0,2,1:T(8,128)} fusion(f32[64,64,256]{2,1,0:T(8,128)S(1)} %fusion.38, f32[64,64,256]{2,1,0:T(8,128)S(1)} %copy-done.8, bf16[256,64,64]{0,2,1:T(8,128)(2,1)S(1)} %bitcast.110, f32[256,64]{0,1:T(8,128)S(1)} %copy-done.14, f32[256,64]{0,1:T(8,128)S(1)} %copy-done.16, f32[256,256]{1,0:T(8,128)S(1)} %fusion.47, ...), kind=kOutput, calls=%fused_computation.32 | convolution fusion | flops 565182464 | bytes 15204608 | tf_op jit(solution)/shard_map/while/body/eval_jaxpr/tsh,shp->thp/dot_general | solution.py:18
  152.2 5.6 %copy.39 = f32[256,4096]{1,0:T(8,128)} copy(f32[256,4096]{0,1:T(8,128)} %bitcast.108) | data formatting | bytes 8388608 | tf_op jit(solution)/shard_map/reshape | solution.py:92
  157.8 4.5 multiply_reduce_fusion.1
  162.3 0.2 copy-done.7
  162.5 3.1 multiply_convert_fusion.4
  165.6 90.0 %all-gather.5.cloned.1.call-done = bf16[2048,4096]{1,0:T(8,128)(2,1)} async-done(((bf16[256,4096]{1,0:T(8,128)(2,1)}), bf16[2048,4096]{1,0:T(8,128)(2,1)}) %all-gather.5.cloned.1.call-update) | async-done | bytes 16777232 | tf_op jit(solution)/shard_map/all_gather | solution.py:99
  255.6 14.5 %convolution_convert_fusion.1 = bf16[2048,512]{1,0:T(8,128)(2,1)} fusion(bf16[2048,4096]{1,0:T(8,128)(2,1)} %all-gather.5.cloned.1.call-done, bf16[4096,512]{1,0:T(8,128)(2,1)} %param.26), kind=kOutput, calls=%fused_computation.48 | convolution fusion | flops 8590983168 | bytes 23068672 | tf_op jit(solution)/shard_map/dot_general | solution.py:98
  270.2 4.7 all-to-all-start
  274.9 0.1 copy.45
  275.0 0.1 eq.29
  275.1 0.1 eq.25
  275.3 1.1 reduce-window.24
  276.5 0.2 slice_reduce_fusion.2
  276.7 0.1 copy.46
  276.9 0.1 mul.206
  277.0 0.1 fusion.41
  277.1 24.4 %all-to-all-done = bf16[8,256,512]{2,1,0:T(8,128)(2,1)} async-done(((bf16[8,256,512]{2,1,0:T(8,128)(2,1)}), bf16[8,256,512]{2,1,0:T(8,128)(2,1)}, u32[]{:S(2)}, u32[]{:S(2)}) %all-to-all-start) | async-done | bytes 2097184 | tf_op jit(solution)/shard_map/all_to_all | solution.py:101
  301.5 2.2 convert_bitcast_fusion
  303.7 0.5 copy.60
  304.2 1.1 copy-done.9
  305.3 0.8 fusion.13
  306.1 1.3 copy-done.3
  307.5 0.6 fusion.15
  308.1 1.3 copy-done.5
  309.4 4.6 broadcast_in_dim.95
  314.1 7.2 %reshape.210 = bf16[512,4096]{1,0:T(8,128)(2,1)} reshape(bf16[256,2,4096]{2,1,0:T(2,128)(2,1)} %broadcast_in_dim.95) | data formatting | bytes 8388608 | tf_op jit(solution)/shard_map/reshape | solution.py:124
  321.3 11.8 %scatter_custom_fusion = bf16[768,4096]{1,0:T(8,128)(2,1)} fusion(s32[512]{0:T(512)S(1)} %bitcast.115, bf16[512,4096]{1,0:T(8,128)(2,1)} %reshape.210, bf16[]{:T(256)} %constant.80.clone.1), kind=kCustom, calls=%fused_computation.46 | custom fusion | bytes 6291968 | tf_op jit(solution)/shard_map/scatter | solution.py:126
  333.1 75.5 %all_to_all.23 = bf16[8,96,4096]{2,1,0:T(8,128)(2,1)S(1)} all-to-all(bf16[8,96,4096]{2,1,0:T(8,128)(2,1)} %bitcast.101), channel_id=1, replica_groups=mesh['seq'=8,'batch'=4] {'seq'}, dimensions={0} | all-to-all | bytes 12582912 | tf_op jit(solution)/shard_map/all_to_all | solution.py:129
  408.6 3.4 fusion.26
  412.0 3.5 fusion.33
  415.5 5.3 convolution_convert_fusion
  420.8 5.0 all-to-all-start.2
  425.8 0.1 copy.44
  426.0 0.2 copy.43
  426.2 0.1 reshape.200
  426.4 0.6 fusion.48
  427.0 3.5 gather_fusion.1
  430.5 0.1 reshape.203
  430.7 0.1 fusion.46
  430.8 0.1 broadcast_divide_fusion
  430.9 66.5 %all-to-all-done.2 = bf16[8,96,4096]{2,1,0:T(8,128)(2,1)} async-done(((bf16[8,96,4096]{2,1,0:T(8,128)(2,1)}), bf16[8,96,4096]{2,1,0:T(8,128)(2,1)}, u32[]{:S(2)}, u32[]{:S(2)}) %all-to-all-start.2) | async-done | bytes 6291488 | tf_op jit(solution)/shard_map/all_to_all | solution.py:138
  497.4 12.2 %gather_fusion = bf16[512,4096]{1,0:T(8,128)(2,1)} fusion(bf16[768,4096]{1,0:T(8,128)(2,1)} %bitcast.28, s32[1024]{0:T(1024)S(1)} %pad_clamp_fusion), kind=kCustom, calls=%fused_computation | custom fusion | bytes 8390656 | tf_op jit(solution)/shard_map/gather | solution.py:141
  509.6 9.7 %reshape.191 = f32[256,2,4096]{2,1,0:T(2,128)} reshape(bf16[512,4096]{1,0:T(8,128)(2,1)} %gather_fusion) | data formatting | bytes 12582912 | tf_op jit(solution)/shard_map/convert_element_type | solution.py:141
  519.3 13.6 %multiply_reduce_fusion = f32[256,4096]{1,0:T(8,128)S(1)} fusion(f32[256,2,4096]{2,1,0:T(2,128)} %reshape.191, f32[256,2]{1,0:T(8,128)S(1)} %broadcast_divide_fusion), kind=kLoop, calls=%fused_computation.7 | loop fusion | flops 3145728 | bytes 12584960 | tf_op jit(solution)/shard_map/reduce_sum | solution.py:142
  532.9 2.0 fusion.16
  (73 shorter events, 0.5 us)
Async XLA Ops:
  6.5 409.0 %copy-start = (bf16[1,384,4096]{2,1,0:T(8,128)(2,1)S(1)}, bf16[1,384,4096]{2,1,0:T(8,128)(2,1)}, u32[]{:S(2)}) copy-start(bf16[1,384,4096]{2,1,0:T(8,128)(2,1)} %param.33) | copy-start | bytes 9437188
  6.5 7.9 %copy-start.12 = (bf16[256,128]{1,0:T(8,128)(2,1)S(1)}, bf16[256,128]{1,0:T(8,128)(2,1)}, u32[]{:S(2)}) copy-start(bf16[256,128]{1,0:T(8,128)(2,1)} %param.19) | copy-start | bytes 196612
  6.5 105.8 %all-gather.7.cloned.1.call-start = ((), (), s32[]{:S(2)}) async-start(), calls=%async_computation.4 | async-start | bytes 18874368 | tf_op jit(solution)/shard_map/all_gather | solution.py:73
  8.5 11.1 %copy-start.13 = (f32[256,64]{0,1:T(8,128)}, f32[256,64]{0,1:T(8,128)S(1)}, u32[]{:S(2)}) copy-start(f32[256,64]{0,1:T(8,128)S(1)} %get-tuple-element.32) | copy-start | bytes 196612
  9.4 10.2 %copy-start.15 = (f32[256,64]{0,1:T(8,128)}, f32[256,64]{0,1:T(8,128)S(1)}, u32[]{:S(2)}) copy-start(f32[256,64]{0,1:T(8,128)S(1)} %bitcast_bitcast_fusion) | copy-start | bytes 196612
  14.4 16.9 %copy-start.11 = (bf16[256,128]{1,0:T(8,128)(2,1)S(1)}, bf16[256,128]{1,0:T(8,128)(2,1)}, u32[]{:S(2)}) copy-start(bf16[256,128]{1,0:T(8,128)(2,1)} %param.20) | copy-start | bytes 196612
  19.6 236.0 %all-gather.5.cloned.1.call-start = ((), (), s32[]{:S(2)}) async-start(), calls=%async_computation.3 | async-start | bytes 18874368 | tf_op jit(solution)/shard_map/all_gather | solution.py:99
  31.6 80.8 %copy-start.17 = (f32[8,64,1,1]{0,2,3,1:T(1,128)S(1)}, f32[8,64,1,1]{0,2,3,1:T(1,128)}, u32[]{:S(2)}) copy-start(f32[8,64,1,1]{0,2,3,1:T(1,128)} %copy.49) | copy-start | bytes 6148
  112.4 32.2 %copy-start.16 = (f32[256,64]{0,1:T(8,128)S(1)}, f32[256,64]{0,1:T(8,128)}, u32[]{:S(2)}) copy-start(f32[256,64]{0,1:T(8,128)} %copy-done.15) | copy-start | bytes 196612
  112.4 32.2 %copy-start.19 = (pred[256,256]{1,0:T(8,128)(4,1)S(1)}, pred[256,256]{1,0:T(8,128)(4,1)}, u32[]{:S(2)}) copy-start(pred[256,256]{1,0:T(8,128)(4,1)} %iota_compare_fusion) | copy-start | bytes 196612
  112.4 32.2 %copy-start.20 = (f32[256,64]{0,1:T(8,128)S(1)}, f32[256,64]{0,1:T(8,128)}, u32[]{:S(2)}) copy-start(f32[256,64]{0,1:T(8,128)} %get-tuple-element.34) | copy-start | bytes 196612
  142.7 2.2 copy-start.8
  142.7 2.9 copy-start.10
  142.7 2.9 copy-start.14
  142.7 2.8 copy-start.26
  152.2 10.2 %copy-start.22 = (f32[4096]{0:T(1024)S(1)}, f32[4096]{0:T(1024)}, u32[]{:S(2)}) copy-start(f32[4096]{0:T(1024)} %param.25) | copy-start | bytes 49156
  157.8 4.5 copy-start.2
  157.8 4.7 copy-start.7
  270.2 4.7 copy-start.21
  270.2 31.3 %all-to-all-start = ((bf16[8,256,512]{2,1,0:T(8,128)(2,1)}), bf16[8,256,512]{2,1,0:T(8,128)(2,1)}, u32[]{:S(2)}, u32[]{:S(2)}) async-start(bf16[8,256,512]{2,1,0:T(8,128)(2,1)} %bitcast.111), calls=%async_computation | async-start | bytes 4194304 | tf_op jit(solution)/shard_map/all_to_all | solution.py:101
  303.7 1.6 copy-start.9
  305.3 2.2 copy-start.23
  306.1 1.3 copy-start.3
  308.1 1.3 copy-start.5
  333.1 75.5 %copy-start.24 = (bf16[1,4096,384]{2,1,0:T(8,128)(2,1)S(1)}, bf16[1,4096,384]{2,1,0:T(8,128)(2,1)}, u32[]{:S(2)}) copy-start(bf16[1,4096,384]{2,1,0:T(8,128)(2,1)} %param.31) | copy-start | bytes 9437188
  408.6 3.4 copy-start.25
  420.8 5.6 %copy-start.6 = (bf16[256,4096]{1,0:T(8,128)(2,1)S(1)}, bf16[256,4096]{1,0:T(8,128)(2,1)}, u32[]{:S(2)}) copy-start(bf16[256,4096]{1,0:T(8,128)(2,1)} %copy-done.5) | copy-start | bytes 6291460
  420.8 5.6 %copy-start.18 = (bf16[4096,8]{0,1:T(8,128)(2,1)S(1)}, bf16[4096,8]{0,1:T(8,128)(2,1)}, u32[]{:S(2)}) copy-start(bf16[4096,8]{0,1:T(8,128)(2,1)} %param.29) | copy-start | bytes 196612
  420.8 76.7 %all-to-all-start.2 = ((bf16[8,96,4096]{2,1,0:T(8,128)(2,1)}), bf16[8,96,4096]{2,1,0:T(8,128)(2,1)}, u32[]{:S(2)}, u32[]{:S(2)}) async-start(bf16[8,96,4096]{2,1,0:T(8,128)(2,1)} %bitcast.105), calls=%async_computation.2 | async-start | bytes 12582912 | tf_op jit(solution)/shard_map/all_to_all | solution.py:138
  519.3 13.6 %copy-start.4 = (bf16[256,4096]{1,0:T(8,128)(2,1)S(1)}, bf16[256,4096]{1,0:T(8,128)(2,1)}, u32[]{:S(2)}) copy-start(bf16[256,4096]{1,0:T(8,128)(2,1)} %copy-done.3) | copy-start | bytes 6291460
  519.3 15.6 %copy-start.1 = (bf16[1,384,4096]{2,1,0:T(8,128)(2,1)S(1)}, bf16[1,384,4096]{2,1,0:T(8,128)(2,1)}, u32[]{:S(2)}) copy-start(bf16[1,384,4096]{2,1,0:T(8,128)(2,1)} %param.33) | copy-start | bytes 9437188
Sparse Core Ops, SparseCore 0:
  19.8 92.5 all-gather.6
  165.8 89.8 all-gather.4
where the time goes:
time: 546 us; the launch traced here: 542 us
  waiting for transfers between devices  258 us (47%)
  blocking collectives  85.7 us (16%)
  matrix products  75.1 us (14%)
  local copies, waits for them, and re-layouts  67.5 us (12%)
  other arithmetic  31.8 us (6%)
  between operations  14 us (3%)
  starting transfers between devices  9.77 us (2%)
    all_gather x1, waiting for transfers between devices, shards(): lax.all_gather(normed, 'seq', axis=0, tiled=True)  90 us
    all_gather x1, waiting for transfers between devices, shards(): lax.all_gather(segment_state[None], 'seq', axis=0, tiled=True)  77.1 us
    all_to_all x1, blocking collectives, shards(): lax.all_to_all(departing_state, 'seq', split_axis=0, concat_axis=0, tiled...  75.5 us
    all_to_all x1, waiting for transfers between devices, shards(): lax.all_to_all(finished, 'seq', split_axis=0, concat_axis=0, tiled=True)  66.5 us
    dot_general x1, matrix products, shards(): jnp.einsum('jh,jhpn->hpn', weights, every_state_list, precision=lax.Preci...  30.3 us
    all_to_all x1, waiting for transfers between devices, shards(): lax.all_to_all(columns, 'seq', split_axis=0, concat_axis=1, tiled=True)  24.4 us
    dot_general x1, matrix products, shards(): jnp.dot(lax.all_gather(normed, 'seq', axis=0, tiled=True), w_out, preferr...  14.5 us
    reduce_sum x1, other arithmetic, shards(): total = hidden_wide + jnp.sum(combine[:, :, None] * fetched, axis=1)  13.6 us
  transfers between devices with their start and end apart: 4, of which 4 were waited for; matrix products, arithmetic and copies ran while one was open for 2% of the time, Pallas kernels for 0%

commit v1 on v0

v1 whole, which is shorter than its diff:
```python
import jax
import jax.numpy as jnp
from jax import lax
from jax.sharding import PartitionSpec as P

GROUP = 256
LOW = 4
HIGHEST = lax.Precision.HIGHEST
F32 = jnp.float32
BF16 = jnp.bfloat16


def three_parts(x):
    first = lax.reduce_precision(x, 8, 7)
    rest = x - first
    second = lax.reduce_precision(rest, 8, 7)
    return first, second, rest - second


def shards(
    ssm_input,
    gate_input,
    b_rows,
    c_rows,
    step_raw,
    step_bias,
    rate_log,
    skip_gain,
    norm_gain,
    w_out,
    residual,
    moe_gain,
    router,
    expert_ids,
    w_gate,
    w_up,
    w_down,
):
    n = lax.axis_size("seq")
    tokens = ssm_input.shape[0]
    inner = ssm_input.shape[1]
    heads = rate_log.shape[0]
    head_width = inner // heads
    state_width = b_rows.shape[1]
    assert tokens == GROUP
    high = n // LOW

    groups = [[a * LOW + b for b in range(LOW)] for a in range(high)]
    w_group = lax.all_gather(w_out, "seq", axis=0, axis_index_groups=groups)

    at = jnp.arange(tokens)
    causal = at[:, None] >= at[None, :]
    step_sizes = jax.nn.softplus(step_raw + step_bias[None, :])
    log_decay = -step_sizes * jnp.exp(rate_log)[None, :]
    running = jnp.dot(causal.astype(F32), log_decay, precision=HIGHEST)
    total = running[-1]
    inputs = ssm_input.reshape(tokens, heads, head_width)

    departing = jnp.exp(total[None, :] - running) * step_sizes
    block_in = (departing[:, :, None] * b_rows.astype(F32)[:, None, :]).astype(BF16)
    update = jnp.einsum("shn,shp->hpn", block_in, inputs, preferred_element_type=F32)
    first, second, third = three_parts(total)
    row = jnp.arange(16)[None, :]
    extra = jnp.where(
        row == 0,
        first[:, None],
        jnp.where(row == 1, second[:, None], jnp.where(row == 2, third[:, None], 0.0)),
    )
    extra = jnp.broadcast_to(extra[:, :, None], (heads, 16, state_width))
    packet = jnp.concatenate([update.astype(BF16), extra.astype(BF16)], axis=1)
    share = heads // n
    packet = packet.reshape(n, share, head_width + 16, state_width)
    packet = lax.all_to_all(packet, "seq", split_axis=0, concat_axis=0, tiled=True)
    logs = jnp.sum(packet[:, :, head_width : head_width + 3, 0].astype(F32), axis=2)
    decays = jnp.exp(logs)
    carried = jnp.zeros((share, head_width, state_width), F32)
    entering = []
    for k in range(n):
        entering.append(carried.astype(BF16))
        carried = decays[k][:, None, None] * carried + packet[k, :, :head_width].astype(F32)
    entering = jnp.stack(entering)
    entering = lax.all_to_all(entering, "seq", split_axis=0, concat_axis=0, tiled=True)
    entering = entering.reshape(inner, state_width)

    scores = jnp.dot(c_rows, b_rows.T, preferred_element_type=F32)
    spread = running[:, None, :] - running[None, :, :]
    fall = jnp.exp(jnp.where(causal[:, :, None], spread, -jnp.inf))
    mixing = (scores[:, :, None] * fall * step_sizes[None, :, :]).astype(BF16)
    intra = jnp.einsum("tsh,shp->thp", mixing, inputs, preferred_element_type=F32)
    intra = intra.reshape(tokens, inner)
    own_head = (jnp.arange(inner)[None, :] // head_width == jnp.arange(heads)[:, None]).astype(F32)
    growth = jnp.dot(jnp.exp(running), own_head, precision=HIGHEST)
    arriving = growth * lax.dot_general(
        c_rows, entering, (((1,), (1,)), ((), ())), preferred_element_type=F32
    )
    ssm_out = intra + arriving + jnp.repeat(skip_gain, head_width)[None, :] * ssm_input.astype(F32)
    gated = ssm_out * jax.nn.silu(gate_input.astype(F32))
    normed = (
        gated
        * lax.rsqrt(jnp.mean(gated * gated, axis=1, keepdims=True) + 1e-05)
        * norm_gain[None, :]
    ).astype(BF16)

    def project(rows):
        parts = [
            jnp.dot(rows, w_group[k], preferred_element_type=F32).astype(BF16) for k in range(LOW)
        ]
        return jnp.concatenate(parts, axis=1)

    position = lax.axis_index("seq")
    mine = position // LOW
    come = [
        lax.ppermute(normed, "seq", [(i, (i + s * LOW) % n) for i in range(n)])
        for s in range(1, high)
    ]
    own = project(normed)
    gone = [
        lax.ppermute(project(come[s - 1]), "seq", [(i, (i - s * LOW) % n) for i in range(n)])
        for s in range(1, high)
    ]
    around = jnp.stack([own] + gone)
    mixer_out = jnp.concatenate(
        [
            lax.dynamic_index_in_dim(around, lax.rem(g - mine + high, high), 0, keepdims=False)
            for g in range(high)
        ],
        axis=1,
    )

    hidden = (residual.astype(F32) + mixer_out.astype(F32)).astype(BF16)
    hidden_wide = hidden.astype(F32)
    moe_input = (
        hidden_wide
        * lax.rsqrt(jnp.mean(hidden_wide * hidden_wide, axis=1, keepdims=True) + 1e-05)
        * moe_gain[None, :]
    ).astype(BF16)
    logits = jnp.dot(moe_input, router, preferred_element_type=F32)
    fanout = expert_ids.shape[1]
    capacity = tokens * fanout * 3 // (2 * n)
    picks = [
        (expert_ids[:, k : k + 1] == jnp.arange(n, dtype=jnp.int32)[None, :]).astype(F32)
        for k in range(fanout)
    ]
    earlier = (at[:, None] > at[None, :]).astype(BF16)
    before = jnp.dot(earlier, sum(picks).astype(BF16), preferred_element_type=F32)
    targets = [
        expert_ids[:, k] * capacity + jnp.sum(before * picks[k], axis=1).astype(jnp.int32)
        for k in range(fanout)
    ]
    powers = [jnp.exp(jnp.sum(logits * pick, axis=1)) for pick in picks]
    whole = sum(powers)
    slots = jnp.arange(n * capacity, dtype=jnp.int32)
    chosen = sum((slots[:, None] == target[None, :]).astype(F32) for target in targets)
    width = moe_input.shape[1]
    batch = jnp.dot(chosen.astype(BF16), moe_input, preferred_element_type=F32).astype(BF16)
    batch = lax.all_to_all(batch, "seq", split_axis=0, concat_axis=0, tiled=True)
    gate_part = jnp.dot(batch, w_gate[0], preferred_element_type=F32)
    up_part = jnp.dot(batch, w_up[0], preferred_element_type=F32)
    expert_hidden = (jax.nn.silu(gate_part) * up_part).astype(BF16)
    result = jnp.dot(expert_hidden, w_down[0], preferred_element_type=F32).astype(BF16)
    returned = lax.all_to_all(result, "seq", split_axis=0, concat_axis=0, tiled=True)
    weights = sum(
        jnp.where(target[:, None] == slots[None, :], (power / whole)[:, None], 0.0)
        for target, power in zip(targets, powers)
    )
    upper = lax.reduce_precision(weights, 8, 7)
    both = jnp.concatenate([upper.astype(BF16), (weights - upper).astype(BF16)], axis=0)
    mixed = jnp.dot(both, returned, preferred_element_type=F32)
    return (hidden_wide + mixed[:tokens] + mixed[tokens:]).astype(BF16)


def solution(mesh):
    rows = P(("batch", "seq"), None)
    experts = P("seq", None, None)
    in_specs = (
        rows,
        rows,
        rows,
        rows,
        rows,
        P(),
        P(),
        P(),
        P(),
        P(None, "seq"),
        rows,
        P(),
        P(),
        rows,
        experts,
        experts,
        experts,
    )
    return jax.shard_map(shards, mesh=mesh, in_specs=in_specs, out_specs=rows, check_vma=False)
```

time: 546 us -> 377 us (0.69)
  waiting for transfers between devices: 258 us -> 167 us
  local copies, waits for them, and re-layouts: 67.5 us -> 13.3 us
  matrix products: 75.1 us -> 65.8 us
  blocking collectives: 85.7 us -> 76.4 us
  other arithmetic: 31.8 us -> 23.6 us
  starting transfers between devices: 9.77 us -> 16.6 us
    all_gather x2 -> x1, waiting for transfers between devices: 167 us -> 0.01 us  [shards(): w_group = lax.all_gather(w_out, 'seq', axis=0, axis_index_groups=groups)]
    ppermute x0 -> x2, waiting for transfers between devices: none -> 52.3 us  [the longest x1 43.9 us: shards(): lax.ppermute(normed, 'seq', [(i, (i + s * LOW) % n) for i in range(n)])]
    all_to_all x2 -> x3, waiting for transfers between devices: 90.9 us -> 114 us  [the longest x1 70.1 us: shards(): lax.all_to_all(result, 'seq', split_axis=0, concat_axis=0, tiled=True)]
    reduce_sum x4 -> x1, other arithmetic: 18.3 us -> 1.09 us  [shards(): jnp.sum(packet[:, :, head_width:head_width + 3, 0].astype(F32), axis=2)]
    gather x4 -> x0, local copies, waits for them, and re-layouts: 15.9 us -> none  [the longest x1 12.2 us: shards(): returned[target].astype(jnp.float32).reshape(tokens_here, fanout, width)]
    scatter x1 -> x0, local copies, waits for them, and re-layouts: 11.8 us -> none  [shards(): jnp.zeros((experts_all * capacity, width), jnp.bfloat16).at[target]]
    all_gather x1 -> x0, blocking collectives: 10.2 us -> none  [shards(): lax.all_gather(slab_total[None], 'seq', axis=0, tiled=True)]
    convert_element_type x2 -> x0, local copies, waits for them, and re-layouts: 10.1 us -> none  [the longest x1 9.66 us: shards(): returned[target].astype(jnp.float32).reshape(tokens_here, fanout, width)]
  transfers between devices with their start and end apart: 4 -> 6, of which waited for: 4 -> 5; matrix products, arithmetic and copies ran while one was open for 2% -> 16% of each run, Pallas kernels for 0% -> 0%
where the time goes in v1:
time: 377 us
  waiting for transfers between devices  167 us (44%)
  blocking collectives  76.4 us (20%)
  matrix products  65.8 us (17%)
  other arithmetic  23.6 us (6%)
  starting transfers between devices  16.6 us (4%)
  between operations  13.9 us (4%)
  local copies, waits for them, and re-layouts  13.3 us (4%)
    all_to_all x1, blocking collectives, shards(): lax.all_to_all(batch, 'seq', split_axis=0, concat_axis=0, tiled=True)  76.4 us
    all_to_all x1, waiting for transfers between devices, shards(): lax.all_to_all(result, 'seq', split_axis=0, concat_axis=0, tiled=True)  70.1 us
    ppermute x1, waiting for transfers between devices, shards(): lax.ppermute(normed, 'seq', [(i, (i + s * LOW) % n) for i in range(n)])  43.9 us
    all_to_all x1, waiting for transfers between devices, shards(): lax.all_to_all(packet, 'seq', split_axis=0, concat_axis=0, tiled=True)  30 us
    dot_general x8, matrix products, project(): jnp.dot(rows, w_group[k], preferred_element_type=F32).astype(BF16)  26.3 us
    all_to_all x1, waiting for transfers between devices, shards(): lax.all_to_all(entering, 'seq', split_axis=0, concat_axis=0, tiled=True)  13.9 us
    unnamed x6, other arithmetic  10.9 us
    ppermute x1, waiting for transfers between devices, shards(): lax.ppermute(project(come[s - 1]), 'seq', [(i, (i - s * LOW) % n) for i i...  8.36 us
  transfers between devices with their start and end apart: 6, of which 5 were waited for; matrix products, arithmetic and copies ran while one was open for 16% of the time, Pallas kernels for 0%

profile of v1, /device:TPU:0, one launch (start us, length us, event | category | flops | bytes accessed | tf_op | source)
XLA Modules:
  0.0 376.5 jit_solution(15448159964977529422)
XLA Ops:
  6.6 0.7 all-gather.3.cloned.1.call-update
  7.3 4.2 %copy.22 = bf16[256,4096]{0,1:T(8,128)(2,1)} copy(bf16[256,4096]{1,0:T(8,128)(2,1)} %param.17) | data formatting | bytes 4194304 | tf_op args[0]
  11.6 0.1 compare_select_fusion
  11.7 0.3 fusion.99
  12.0 0.2 slice_reduce_fusion
  12.2 0.1 select_convert_fusion
  12.3 0.1 exponential_multiply_fusion
  12.5 4.2 %fusion.46 = bf16[64,64,128]{2,1,0:T(8,128)(2,1)S(1)} fusion(bf16[256,64,64]{0,2,1:T(8,128)(2,1)} %bitcast.79, f32[256,128]{1,0:T(8,128)S(1)} %convert_element_type.223, f32[256,64]{0,1:T(8,128)S(1)} %exponential_multiply_fusion), kind=kOutput, calls=%fused_computation.62 | convolution fusion | flops 273154048 | bytes 3342336 | tf_op jit(solution)/shard_map/shn,shp->hpn/dot_general | solution.py:61
  16.6 0.2 broadcast_in_dim.132
  16.8 1.2 pad_maximum_fusion
  18.0 5.2 %all-to-all-start = ((bf16[8,8,80,128]{3,2,1,0:T(8,128)(2,1)}), bf16[8,8,80,128]{3,2,1,0:T(8,128)(2,1)}, u32[]{:S(2)}, u32[]{:S(2)}) async-start(bf16[8,8,80,128]{3,2,1,0:T(8,128)(2,1)} %bitcast.77), calls=%async_computation | async-start | bytes 2621440 | tf_op jit(solution)/shard_map/all_to_all | solution.py:73
  23.2 0.6 iota_compare_fusion.7
  23.8 0.7 broadcast_dynamic-update-slice_fusion
  24.5 1.0 fusion.113
  25.5 30.0 %all-to-all-done = bf16[8,8,80,128]{3,2,1,0:T(8,128)(2,1)} async-done(((bf16[8,8,80,128]{3,2,1,0:T(8,128)(2,1)}), bf16[8,8,80,128]{3,2,1,0:T(8,128)(2,1)}, u32[]{:S(2)}, u32[]{:S(2)}) %all-to-all-start) | async-done | bytes 1310752 | tf_op jit(solution)/shard_map/all_to_all | solution.py:73
  55.5 1.1 convert_reduce_fusion
  56.6 1.7 fusion.97
  58.3 1.8 fusion.96
  60.1 1.8 convert_dynamic-update-slice_fusion.1
  61.9 1.9 fusion.95
  63.8 2.1 convert_dynamic-update-slice_fusion
  65.9 1.7 fusion.94
  67.6 1.7 fusion.98
  69.3 4.2 %all-to-all-start.1 = ((bf16[8,8,64,128]{3,2,1,0:T(8,128)(2,1)}), bf16[8,8,64,128]{3,2,1,0:T(8,128)(2,1)}, u32[]{:S(2)}, u32[]{:S(2)}) async-start(bf16[8,8,64,128]{3,2,1,0:T(8,128)(2,1)} %fusion.98), calls=%async_computation.1 | async-start | bytes 2097152 | tf_op jit(solution)/shard_map/all_to_all | solution.py:82
  73.6 7.2 %fusion = f32[64,256,64]{1,2,0:T(8,128)} fusion(bf16[256,64,64]{0,2,1:T(8,128)(2,1)} %bitcast.80, f32[256,64]{0,1:T(8,128)} %copy-done.9, f32[256,64]{0,1:T(8,128)S(1)} %fusion.99, f32[256,256]{1,0:T(8,128)S(1)} %fusion.113, pred[256,256]{1,0:T(8,128)(4,1)} %iota_compare_fusion.7), kind=kOutput, calls=%fused_computation.1 | convolution fusion | flops 557842432 | bytes 6750208 | tf_op jit(solution)/shard_map/tsh,shp->thp/dot_general | solution.py:89
  80.8 5.6 %copy.24 = f32[256,4096]{1,0:T(8,128)} copy(f32[256,4096]{0,1:T(8,128)} %bitcast.78) | data formatting | bytes 8388608 | tf_op jit(solution)/shard_map/reshape | solution.py:90
  86.4 0.1 broadcast_in_dim.134
  86.5 0.1 mul.262
  86.6 13.9 %all-to-all-done.1 = bf16[8,8,64,128]{3,2,1,0:T(8,128)(2,1)} async-done(((bf16[8,8,64,128]{3,2,1,0:T(8,128)(2,1)}), bf16[8,8,64,128]{3,2,1,0:T(8,128)(2,1)}, u32[]{:S(2)}, u32[]{:S(2)}) %all-to-all-start.1) | async-done | bytes 1048608 | tf_op jit(solution)/shard_map/all_to_all | solution.py:82
  100.5 2.1 convolution_bitcast_fusion
  102.6 0.4 copy-done.3
  103.0 0.7 copy-done.4
  103.7 0.6 copy-done.18
  104.3 3.7 multiply_reduce_fusion
  108.1 1.9 multiply_convert_fusion.4
  110.0 0.5 collective-permute-start
  110.5 43.9 %collective-permute-done = bf16[256,4096]{1,0:T(8,128)(2,1)} collective-permute-done((bf16[256,4096]{1,0:T(8,128)(2,1)}, bf16[256,4096]{1,0:T(8,128)(2,1)}, u32[]{:S(2)}, u32[]{:S(2)}) %collective-permute-start) | collective-permute-done | bytes 2097184 | tf_op jit(solution)/shard_map/ppermute | solution.py:113
  154.4 4.2 %fusion.50 = bf16[256,512]{1,0:T(8,128)(2,1)S(1)} fusion(bf16[256,4096]{1,0:T(8,128)(2,1)} %collective-permute-done, bf16[16384,512]{1,0:T(8,128)(2,1)} %all-gather.3.cloned.1.call-done), kind=kOutput, calls=%fused_computation.65 | convolution fusion | flops 1073872896 | bytes 6553600 | tf_op jit(solution)/shard_map/dot_general | solution.py:106
  158.7 4.8 %fusion.56 = bf16[256,512]{1,0:T(8,128)(2,1)S(1)} fusion(bf16[256,4096]{1,0:T(8,128)(2,1)} %collective-permute-done, bf16[16384,512]{1,0:T(8,128)(2,1)} %all-gather.3.cloned.1.call-done), kind=kOutput, calls=%fused_computation.67 | convolution fusion | flops 1073872896 | bytes 6553600 | tf_op jit(solution)/shard_map/dot_general | solution.py:106
  163.5 0.4 copy-done.15
  163.9 2.9 fusion.62
  166.8 2.9 fusion.68
  169.7 0.1 pad_maximum_fusion.1
  169.8 1.7 collective-permute-start.1
  171.5 2.9 fusion.53
  174.4 2.9 fusion.59
  177.3 2.9 fusion.65
  180.2 2.9 fusion.71
  183.1 0.1 maximum_bitcast_fusion
  183.2 8.4 %collective-permute-done.1 = bf16[256,2048]{1,0:T(8,128)(2,1)S(1)} collective-permute-done((bf16[256,2048]{1,0:T(8,128)(2,1)S(1)}, bf16[256,2048]{1,0:T(8,128)(2,1)S(1)}, u32[]{:S(2)}, u32[]{:S(2)}) %collective-permute-start.1) | collective-permute-done | bytes 1048608 | tf_op jit(solution)/shard_map/ppermute | solution.py:118
  191.6 0.7 fusion.77
  192.3 1.2 fusion.13
  193.6 0.7 fusion.84
  194.3 0.2 select_reduce_fusion.3
  194.5 2.0 convolution_convert_fusion
  196.6 76.4 %all_to_all.34 = bf16[8,96,4096]{2,1,0:T(8,128)(2,1)S(1)} all-to-all(bf16[8,96,4096]{2,1,0:T(8,128)(2,1)S(1)} %bitcast.73), channel_id=1, replica_groups=mesh['seq'=8,'batch'=4] {'seq'}, dimensions={0} | all-to-all | bytes 12582912 | tf_op jit(solution)/shard_map/all_to_all | solution.py:156
  273.0 3.4 fusion.40
  276.4 3.5 fusion.47
  279.9 5.4 %convolution_convert_fusion.1 = bf16[768,4096]{1,0:T(8,128)(2,1)} fusion(bf16[768,384]{1,0:T(8,128)(2,1)S(1)} %fusion.47, bf16[1,384,4096]{2,1,0:T(8,128)(2,1)S(1)} %copy-done), kind=kOutput, calls=%fused_computation.10 | convolution fusion | flops 2419064832 | bytes 10027008 | tf_op jit(solution)/shard_map/dot_general | solution.py:160
  285.3 5.0 %all-to-all-start.3 = ((bf16[8,96,4096]{2,1,0:T(8,128)(2,1)}), bf16[8,96,4096]{2,1,0:T(8,128)(2,1)}, u32[]{:S(2)}, u32[]{:S(2)}) async-start(bf16[8,96,4096]{2,1,0:T(8,128)(2,1)} %bitcast.74), calls=%async_computation.3 | async-start | bytes 12582912 | tf_op jit(solution)/shard_map/all_to_all | solution.py:161
  290.4 1.2 reduce-precision_convert_fusion
  291.6 70.1 %all-to-all-done.3 = bf16[8,96,4096]{2,1,0:T(8,128)(2,1)} async-done(((bf16[8,96,4096]{2,1,0:T(8,128)(2,1)}), bf16[8,96,4096]{2,1,0:T(8,128)(2,1)}, u32[]{:S(2)}, u32[]{:S(2)}) %all-to-all-start.3) | async-done | bytes 6291488 | tf_op jit(solution)/shard_map/all_to_all | solution.py:161
  361.7 5.7 %fusion.79 = f32[512,4096]{1,0:T(8,128)S(1)} fusion(bf16[768,4096]{1,0:T(8,128)(2,1)} %bitcast.30, bf16[256,768]{1,0:T(8,128)(2,1)} %get-tuple-element.18, bf16[256,768]{1,0:T(8,128)(2,1)S(1)} %get-tuple-element.17), kind=kOutput, calls=%fused_computation.83 | convolution fusion | flops 3222798336 | bytes 15466496 | tf_op jit(solution)/shard_map/dot_general | solution.py:168
  367.4 2.3 fusion.17
  (57 shorter events, 0.3 us)
Async XLA Ops:
  6.5 273.4 %copy-start = (bf16[1,384,4096]{2,1,0:T(8,128)(2,1)S(1)}, bf16[1,384,4096]{2,1,0:T(8,128)(2,1)}, u32[]{:S(2)}) copy-start(bf16[1,384,4096]{2,1,0:T(8,128)(2,1)} %param.33) | copy-start | bytes 9437188
  6.5 0.8 copy-start.20
  6.5 5.0 %copy-start.8 = (bf16[256,128]{1,0:T(8,128)(2,1)S(1)}, bf16[256,128]{1,0:T(8,128)(2,1)}, u32[]{:S(2)}) copy-start(bf16[256,128]{1,0:T(8,128)(2,1)} %param.19) | copy-start | bytes 196612
  6.5 5.1 %copy-start.7 = (f32[256,64]{0,1:T(8,128)S(1)}, f32[256,64]{0,1:T(8,128)}, u32[]{:S(2)}) copy-start(f32[256,64]{0,1:T(8,128)} %param.21) | copy-start | bytes 196612
  6.5 5.1 %copy-start.13 = (f32[64]{0:T(128)S(1)}, f32[64]{0:T(128)}, u32[]{:S(2)}) copy-start(f32[64]{0:T(128)} %param.22) | copy-start | bytes 772
  6.5 147.9 %all-gather.3.cloned.1.call-start = ((), (), s32[]{:S(2)}) async-start(), calls=%async_computation.4 | async-start | bytes 20971520 | tf_op jit(solution)/shard_map/all_gather | solution.py:49
  11.7 0.7 copy-start.9
  16.6 7.8 %copy-start.6 = (bf16[256,128]{1,0:T(8,128)(2,1)S(1)}, bf16[256,128]{1,0:T(8,128)(2,1)}, u32[]{:S(2)}) copy-start(bf16[256,128]{1,0:T(8,128)(2,1)} %param.20) | copy-start | bytes 196612
  18.0 37.5 %all-to-all-start = ((bf16[8,8,80,128]{3,2,1,0:T(8,128)(2,1)}), bf16[8,8,80,128]{3,2,1,0:T(8,128)(2,1)}, u32[]{:S(2)}, u32[]{:S(2)}) async-start(bf16[8,8,80,128]{3,2,1,0:T(8,128)(2,1)} %bitcast.77), calls=%async_computation | async-start | bytes 2621440 | tf_op jit(solution)/shard_map/all_to_all | solution.py:73
  69.3 31.2 %all-to-all-start.1 = ((bf16[8,8,64,128]{3,2,1,0:T(8,128)(2,1)}), bf16[8,8,64,128]{3,2,1,0:T(8,128)(2,1)}, u32[]{:S(2)}, u32[]{:S(2)}) async-start(bf16[8,8,64,128]{3,2,1,0:T(8,128)(2,1)} %fusion.98), calls=%async_computation.1 | async-start | bytes 2097152 | tf_op jit(solution)/shard_map/all_to_all | solution.py:82
  80.8 5.6 %copy-start.14 = (f32[64]{0:T(128)S(1)}, f32[64]{0:T(128)}, u32[]{:S(2)}) copy-start(f32[64]{0:T(128)} %param.24) | copy-start | bytes 772
  100.5 2.5 copy-start.3
  100.5 3.2 copy-start.4
  100.5 3.8 %copy-start.18 = (bf16[256,4096]{1,0:T(8,128)(2,1)S(1)}, bf16[256,4096]{1,0:T(8,128)(2,1)}, u32[]{:S(2)}) copy-start(bf16[256,4096]{1,0:T(8,128)(2,1)} %param.18) | copy-start | bytes 6291460
  104.3 3.7 copy-start.10
  108.0 2.5 copy-start.12
  110.0 44.5 %collective-permute-start = (bf16[256,4096]{1,0:T(8,128)(2,1)}, bf16[256,4096]{1,0:T(8,128)(2,1)}, u32[]{:S(2)}, u32[]{:S(2)}) collective-permute-start(bf16[256,4096]{1,0:T(8,128)(2,1)} %multiply_convert_fusion.4), channel_id=1, source_target_pairs={{0,16},{4,20},{8,24},{12,28},{16,0},{20,4},{24,8},{28,12},{1,17},{... | collective-permute-start | bytes 6291464 | tf_op jit(solution)/shard_map/ppermute | solution.py:113
  154.4 9.5 %copy-start.15 = (bf16[16384,512]{1,0:T(8,128)(2,1)S(1)}, bf16[16384,512]{1,0:T(8,128)(2,1)}, u32[]{:S(2)}) copy-start(bf16[16384,512]{1,0:T(8,128)(2,1)} %all-gather.3.cloned.1.call-done) | copy-start | bytes 50331652
  169.8 21.7 %collective-permute-start.1 = (bf16[256,2048]{1,0:T(8,128)(2,1)S(1)}, bf16[256,2048]{1,0:T(8,128)(2,1)S(1)}, u32[]{:S(2)}, u32[]{:S(2)}) collective-permute-start(bf16[256,2048]{1,0:T(8,128)(2,1)S(1)} %pad_maximum_fusion.1), channel_id=1, source_target_pairs={{0,16},{4,20},{8,24},{12,28},{16,0},{20,4},{24,8},{28,12},{1,17},{... | collective-permute-start | bytes 3145736 | tf_op jit(solution)/shard_map/ppermute | solution.py:118
  183.1 9.3 %copy-start.5 = (bf16[256,4096]{1,0:T(8,128)(2,1)S(1)}, bf16[256,4096]{1,0:T(8,128)(2,1)}, u32[]{:S(2)}) copy-start(bf16[256,4096]{1,0:T(8,128)(2,1)} %param.27) | copy-start | bytes 6291460
  192.3 1.2 copy-start.11
  192.3 1.2 copy-start.19
  193.5 3.0 copy-start.1
  196.6 76.4 %copy-start.16 = (bf16[1,4096,384]{2,1,0:T(8,128)(2,1)S(1)}, bf16[1,4096,384]{2,1,0:T(8,128)(2,1)}, u32[]{:S(2)}) copy-start(bf16[1,4096,384]{2,1,0:T(8,128)(2,1)} %param.31) | copy-start | bytes 9437188
  273.0 3.4 copy-start.17
  285.3 76.3 %all-to-all-start.3 = ((bf16[8,96,4096]{2,1,0:T(8,128)(2,1)}), bf16[8,96,4096]{2,1,0:T(8,128)(2,1)}, u32[]{:S(2)}, u32[]{:S(2)}) async-start(bf16[8,96,4096]{2,1,0:T(8,128)(2,1)} %bitcast.74), calls=%async_computation.3 | async-start | bytes 12582912 | tf_op jit(solution)/shard_map/all_to_all | solution.py:161
  361.7 5.7 %copy-start.2 = (bf16[256,4096]{1,0:T(8,128)(2,1)S(1)}, bf16[256,4096]{1,0:T(8,128)(2,1)}, u32[]{:S(2)}) copy-start(bf16[256,4096]{1,0:T(8,128)(2,1)} %copy-done.1) | copy-start | bytes 6291460
Sparse Core Ops, SparseCore 0:
  8.9 133.8 all-gather.2
